TPU v7x, 512 devices: a whole 4x4x16 slice. The times are simulated.
512 devices in a mesh: dp: 64 (over y_hi, z, core), mp: 8 (over x, y_lo).
Axes of the slice: x: 4, y: 4 (y_hi: 2, y_lo: 2; y = y_hi * 2 + y_lo), z: 16, core: 2. Of those that a mesh axis runs over, the one named last changes fastest.
Arguments:
- tokens: bfloat16 [32768, 4096], P(('dp', 'mp')), may hold values from -6 to 6
- key_grad: bfloat16 [32768, 1024], P('dp', 'mp'), may hold values from -6 to 6
- key_weight: bfloat16 [4096, 1024], P(None, 'mp'), may hold values from -0.1875 to 0.1875
- momentum: bfloat16 [64, 4096, 1024], P('dp', None, 'mp'), may hold values from -4 to 4
- band_freqs: int32 [2, 16], replicated, may hold values from 0 to 31, as said below
Outputs:
- new_momentum: bfloat16 [64, 4096, 1024], P('dp', None, 'mp')
- update: bfloat16 [4096, 1024], P(None, 'mp')
- input_grad: bfloat16 [32768, 4096], P(('dp', 'mp'))
Inputs may be any that keep to these rules, and one draw needn't show every extreme that they name: `band_freqs`: each row holds 16 distinct frequencies in increasing order, the first 0 and the last 31.
All inputs are finite; a program needn't handle non-finite values.
Results may differ from a plain program's by a relative error of at most 0.017.
Values may be sent and summed in bfloat16 or wider, within the bound.
A program may use at most 128 MiB of HBM per device.

v0:
```python
import math

import jax
import jax.numpy as jnp
from jax import lax
from jax.sharding import PartitionSpec as P

SPAN = 64


momentum_decay = 0.999
exact_mode = lax.Precision.HIGHEST


def cosine_table(count):
    freq_idx = jnp.arange(count, dtype=jnp.float32)[:, None]
    cell_idx = jnp.arange(count, dtype=jnp.float32)[None, :]
    cosines = jnp.cos(math.pi * (2.0 * cell_idx + 1.0) * freq_idx / (2.0 * count))
    scales = jnp.where(freq_idx == 0.0, math.sqrt(1.0 / count), math.sqrt(2.0 / count))
    return cosines * scales


def pick_rows(cosines, freqs):
    selector = freqs[:, None] == jnp.arange(cosines.shape[0], dtype=jnp.int32)[None, :]
    return jnp.sum(jnp.where(selector[:, :, None], cosines[None, :, :], jnp.float32(0.0)), axis=1)


def forward_band(moment, row_basis, col_basis):
    row_blocks = moment.shape[0] // SPAN
    col_blocks = moment.shape[1] // SPAN
    blocks = moment.reshape(row_blocks, SPAN, col_blocks, SPAN)
    left_done = jnp.einsum("ia,racb->ricb", row_basis, blocks, precision=exact_mode)
    return jnp.einsum("ricb,jb->ricj", left_done, col_basis, precision=exact_mode)


def inverse_band(band_coef, row_basis, col_basis):
    left_done = jnp.einsum("ricj,ia->racj", band_coef, row_basis, precision=exact_mode)
    blocks = jnp.einsum("racj,jb->racb", left_done, col_basis, precision=exact_mode)
    return blocks.reshape(blocks.shape[0] * SPAN, blocks.shape[2] * SPAN)


def per_device(tokens, key_grad, key_weight, momentum, band_freqs):
    replica_rows = key_grad.shape[0]
    key_rows = key_grad
    summed_grad = lax.psum_scatter(
        lax.dot_general(
            key_rows, key_weight, (((1,), (1,)), ((), ())), preferred_element_type=jnp.float32
        ).astype(jnp.bfloat16),
        "mp",
        scatter_dimension=0,
        tiled=True,
    )
    key_rows = key_grad
    gradient = (
        lax.dot_general(
            lax.all_gather(tokens, "mp", axis=0, tiled=True),
            key_rows,
            (((0,), (0,)), ((), ())),
            preferred_element_type=jnp.float32,
        )
        / replica_rows
    )
    moment = momentum_decay * momentum[0].astype(jnp.float32) + gradient
    cosines = cosine_table(SPAN)
    row_basis = pick_rows(cosines, band_freqs[0])
    col_basis = pick_rows(cosines, band_freqs[1])
    band_coef = forward_band(moment, row_basis, col_basis)
    sent_band = lax.optimization_barrier(band_coef.astype(jnp.bfloat16))
    own_part = inverse_band(sent_band.astype(jnp.float32), row_basis, col_basis)
    new_momentum = (moment - own_part).astype(jnp.bfloat16)[None]
    flat_band = sent_band.reshape(1, -1)
    summed = jnp.sum(
        lax.all_gather(flat_band, "dp", axis=0, tiled=True).astype(jnp.float32), axis=0
    )
    update = inverse_band(summed.reshape(band_coef.shape), row_basis, col_basis).astype(
        jnp.bfloat16
    )
    return (new_momentum, update, summed_grad)


def solution(mesh):
    placed = (P(("dp", "mp"), None), P("dp", "mp"), P(None, "mp"), P("dp", None, "mp"), P())
    return jax.shard_map(
        per_device,
        mesh=mesh,
        in_specs=placed,
        out_specs=(P("dp", None, "mp"), P(None, "mp"), P(("dp", "mp"), None)),
        check_vma=False,
    )
```

profile of v0, /device:TPU:1, one launch (start us, length us, event | category | flops | bytes accessed | tf_op | source)
XLA Modules:
  0.0 401.8 jit_solution(3581501854543302886)
XLA Ops:
  7.2 0.0 copy-start
  7.2 0.0 all-gather.4.cloned.1.call-start
  7.2 0.7 all-gather.4.cloned.1.call-update
  7.9 0.0 all-gather.6.cloned.1.call-start
  8.0 0.8 slice_bitcast_fusion.1
  8.7 0.1 iota_compare_fusion
  8.8 0.1 cosine_multiply_fusion
  8.9 0.4 select_reduce_fusion
  9.3 103.5 %all-gather.4.cloned.1.call-done = bf16[512,4096]{1,0:T(8,128)(2,1)} async-done(((bf16[64,4096]{1,0:T(8,128)(2,1)}), bf16[512,4096]{1,0:T(8,128)(2,1)}) %all-gather.4.cloned.1.call-update) | async-done | bytes 4194320 | tf_op jit(solution)/shard_map/all_gather | solution.py:56
  112.8 3.8 fusion
  116.7 3.7 reshape.122
  120.4 0.0 copy-start.1
  120.4 4.5 %fusion.3 = f32[64,16,2,64]{3,1,2,0:T(8,128)S(1)} fusion(f32[64,64,2,64]{3,2,1,0:T(2,128)} %reshape.122, f32[16,64]{1,0:T(8,128)S(1)} %get-tuple-element.13), kind=kOutput, calls=%fused_computation.8 | convolution fusion | flops 100663296 | bytes 2625536 | tf_op jit(solution)/shard_map/ia,racb->ricb/dot_general | solution.py:32
  124.8 3.0 convolution_convert_fusion.2
  127.8 1.2 copy.28
  129.0 2.1 reshape.126
  131.1 0.0 all-gather.6.cloned.1.call-update
  131.1 0.2 reduce-scatter.2.cloned.1.call-start
  131.4 0.0 copy-done
  131.4 0.0 copy-done.1
  131.4 3.2 convolution_convert_fusion
  134.6 0.0 reduce-scatter.2.cloned.1.call-update
  134.6 1.6 convolution_bitcast_fusion.1
  136.2 3.0 copy.26
  139.2 8.0 %fusion.10 = f32[64,64,2,64]{3,1,2,0:T(8,128)S(1)} fusion(f32[64,64,2,16]{1,3,2,0:T(8,128)} %copy.26, f32[16,64]{1,0:T(8,128)S(1)} %get-tuple-element.12), kind=kOutput, calls=%fused_computation.19 | convolution fusion | flops 100663296 | bytes 2625536 | tf_op jit(solution)/shard_map/racj,jb->racb/dot_general | solution.py:38
  147.2 6.0 %copy.27 = f32[64,64,2,64]{3,2,1,0:T(2,128)} copy(f32[64,64,2,64]{3,1,2,0:T(8,128)S(1)} %fusion.10) | data formatting | bytes 4194304 | tf_op jit(solution)/shard_map/racj,jb->racb/dot_general | solution.py:38
  153.2 5.4 %reshape.123 = f32[4096,128]{1,0:T(8,128)} reshape(f32[64,64,2,64]{3,2,1,0:T(2,128)} %copy.27) | data formatting | bytes 4194304 | tf_op jit(solution)/shard_map/reshape | solution.py:39
  158.6 2.8 fusion.6
  161.4 138.0 %all-gather.6.cloned.1.call-done = bf16[64,1,32768]{2,1,0:T(2,128)(2,1)} async-done(((bf16[1,1,32768]{2,1,0:T(2,128)(2,1)}), bf16[64,1,32768]{2,1,0:T(2,128)(2,1)}) %all-gather.6.cloned.1.call-update) | async-done | bytes 4194320 | tf_op jit(solution)/shard_map/all_gather | solution.py:73
  299.3 8.8 %convert_reduce_fusion = f32[32768]{0:T(1024)S(1)} fusion(bf16[64,1,32768]{2,1,0:T(2,128)(2,1)} %all-gather.6.cloned.1.call-done), kind=kLoop, calls=%fused_computation | loop fusion | flops 4161536 | bytes 4325376 | tf_op jit(solution)/shard_map/reduce_sum | solution.py:72
  308.2 1.4 reshape.125
  309.5 0.6 copy.29
  310.1 1.0 convolution_bitcast_fusion
  311.1 0.9 copy.30
  312.1 6.9 %convolution_convert_fusion.1 = bf16[64,64,2,64]{3,1,2,0:T(8,128)(2,1)S(1)} fusion(f32[64,64,2,16]{1,3,2,0:T(8,128)S(1)} %copy.30, f32[16,64]{1,0:T(8,128)S(1)} %get-tuple-element.12), kind=kOutput, calls=%fused_computation.7 | convolution fusion | flops 101187584 | bytes 1576960 | tf_op jit(solution)/shard_map/racj,jb->racb/dot_general | solution.py:38
  319.0 2.2 copy.35
  321.2 1.8 reshape.132
  323.0 72.3 %reduce-scatter.2.cloned.1.call-done = bf16[64,4096]{1,0:T(8,128)(2,1)} async-done(((bf16[512,4096]{1,0:T(8,128)(2,1)}), bf16[64,4096]{1,0:T(8,128)(2,1)}) %reduce-scatter.2.cloned.1.call-update) | async-done | bytes 524304 | tf_op jit(solution)/shard_map/reduce_scatter | solution.py:45
  (1 shorter events, 0.0 us)
Async XLA Ops:
  7.2 124.2 %copy-start = (bf16[4096,128]{1,0:T(8,128)(2,1)S(1)}, bf16[4096,128]{1,0:T(8,128)(2,1)}, u32[]{:S(2)}) copy-start(bf16[4096,128]{1,0:T(8,128)(2,1)} %param.7) | copy-start | bytes 3145732
  7.2 105.7 %all-gather.4.cloned.1.call-start = ((), (), s32[]{:S(2)}) async-start(), calls=%async_computation.1 | async-start | bytes 4718592 | tf_op jit(solution)/shard_map/all_gather | solution.py:56
  7.9 291.4 %all-gather.6.cloned.1.call-start = ((), (), s32[]{:S(2)}) async-start(), calls=%async_computation.3 | async-start | bytes 8519680 | tf_op jit(solution)/shard_map/all_gather | solution.py:73
  120.4 11.0 %copy-start.1 = (bf16[512,128]{1,0:T(8,128)(2,1)S(1)}, bf16[512,128]{1,0:T(8,128)(2,1)}, u32[]{:S(2)}) copy-start(bf16[512,128]{1,0:T(8,128)(2,1)} %param.6) | copy-start | bytes 393220
  131.1 264.1 %reduce-scatter.2.cloned.1.call-start = ((), (), s32[]{:S(2)}) async-start(), calls=%async_computation.2 | async-start | bytes 4718592 | tf_op jit(solution)/shard_map/reduce_scatter | solution.py:45
Sparse Core Ops, SparseCore 0:
  10.1 102.6 all-gather.3
  131.2 168.0 all-gather.5
  302.7 92.4 reduce-scatter.1
where the time goes:
time: 402 us
  waiting for transfers between devices  314 us (78%)
  matrix products  32.1 us (8%)
  local copies, waits for them, and re-layouts  28.9 us (7%)
  between operations  13.9 us (3%)
  other arithmetic  12.2 us (3%)
    all_gather x1, waiting for transfers between devices, per_device(): lax.all_gather(flat_band, 'dp', axis=0, tiled=True).astype(jnp.float32)  138 us
    all_gather x1, waiting for transfers between devices, per_device(): lax.all_gather(tokens, 'mp', axis=0, tiled=True)  104 us
    reduce_scatter x1, waiting for transfers between devices, per_device(): lax.psum_scatter(lax.dot_general(key_rows, key_weight, (((1,), (1,)), (()...  72.3 us
    dot_general x2, matrix products, inverse_band(): jnp.einsum('racj,jb->racb', left_done, col_basis, precision=exact_mode)  15 us
    reduce_sum x1, other arithmetic, per_device(): jnp.sum(lax.all_gather(flat_band, 'dp', axis=0, tiled=True).astype(jnp.fl...  8.84 us
  transfers between devices with their start and end apart: 3, of which 3 were waited for; matrix products, arithmetic and copies ran while one was open for 14% of the time, Pallas kernels for 0%

commit v1 on v0

v1 whole, which is shorter than its diff:
```python
import functools
import math

import jax
import jax.numpy as jnp
import numpy as np
from jax import lax
from jax.experimental import pallas as pl
from jax.experimental.pallas import tpu as pltpu
from jax.sharding import PartitionSpec as P

MESH = pl.DeviceIdType.MESH
SPAN = 64
BAND = 16
DECAY = 0.999
N_X, N_Z = 4, 16
CHUNKS = 4
GROUP = 256
TOK = 64
BF = jnp.bfloat16
F32 = jnp.float32


def split(value):
    high = value.astype(BF)
    return high, (value - high.astype(F32)).astype(BF)


def mm(a, b, dims=((1,), (0,))):
    return lax.dot_general(a, b, (dims, ((), ())), preferred_element_type=F32)


def kernel(
    tok, kg, kw, mom, left_w, right_w, inv_right_w, inv_left_w,
    new_mom, update, in_grad,
    t_all, k_cat, k_rows, w_all, g_own, g_send, g_recv, c_send, s1, s2, s3, packed, p_own, p_send, p_recv,
    loc_sem, ks, kr, ts, tr, ws, wr, cs, cr, gs, gr, ps, pr, s1s, s1r, s2s, s2r, s3s, s3r, z_sem,
):
    width = t_all.shape[3]
    groups = width // GROUP
    dp, mp = lax.axis_index("dp"), lax.axis_index("mp")
    yh, z, core = dp // 32, (dp // 2) % N_Z, dp % 2
    x, yl = mp // 2, mp % 2
    part = yh * 2 + core

    def device(x=x, yl=yl, yh=yh, z=z, core=core):
        return (yh * 32 + z * 2 + core, x * 2 + yl)

    def x_at(step):
        return (x + N_X + step) % N_X

    def z_at(step):
        return (z + N_Z + step) % N_Z

    right, left, across = x_at(1), x_at(-1), x_at(2)
    sent = []

    def send(src, dst, send_sem, recv_sem, to):
        copy = pltpu.make_async_remote_copy(
            src_ref=src, dst_ref=dst, send_sem=send_sem, recv_sem=recv_sem, device_id=to, device_id_type=MESH
        )
        copy.start()
        sent.append(copy)
        return copy

    def lanes(i):
        return pl.ds(pl.multiple_of(i * 128, 128), 128)

    near = [device(x=right), device(x=left), device(x=across), device(z=z_at(1)), device(z=z_at(-1))]
    for o in range(1, 8):
        other = (yl * 4 + part + o) % 8
        near.append(device(yl=other // 4, yh=(other // 2) % 2, core=other % 2))
    barrier = pltpu.get_barrier_semaphore()
    for peer in near:
        pl.semaphore_signal(barrier, inc=1, device_id=peer, device_id_type=MESH)

    mine = pl.ds(pl.multiple_of(yl * TOK, TOK), TOK)
    theirs = pl.ds(pl.multiple_of((1 - yl) * TOK, TOK), TOK)
    local = [pltpu.make_async_copy(kg.at[:, mine], k_cat.at[:, :, pl.ds(0, 128)], loc_sem.at[0]),
             pltpu.make_async_copy(kg.at[x, mine], k_rows.at[0, :, lanes(x)], loc_sem.at[1]),
             pltpu.make_async_copy(kg.at[x, theirs], k_rows.at[1, :, lanes(x)], loc_sem.at[2]),
             pltpu.make_async_copy(kw, w_all.at[:, lanes(x)], loc_sem.at[3])]
    for c in range(CHUNKS):
        local.append(pltpu.make_async_copy(tok.at[:, pl.ds(c * width, width)], t_all.at[c, x], loc_sem.at[4 + c]))
    for copy in local:
        copy.start()
    pl.semaphore_wait(barrier, len(near))

    half = width // 2

    def token_piece(c, owner, rows=None):
        return t_all.at[c, owner] if rows is None else t_all.at[c, owner, rows]

    def weight_piece(c, owner, start=0, count=half):
        first = pl.multiple_of(c * width + core * half + start, 16)
        return w_all.at[pl.ds(first, count), lanes(owner)]

    def send_item(s):
        if s < CHUNKS:
            src, dst, ss, rs = tok.at[:, pl.ds(s * width, width)], token_piece(s, x), ts.at[s], tr.at[s]
        else:
            c = s - CHUNKS
            src = kw.at[pl.ds(pl.multiple_of(c * width + core * half, 16), half)]
            dst, ss, rs = weight_piece(c, x), ws.at[c], wr.at[c]
        return (send(src, dst, ss.at[0], rs.at[0], device(x=right)), send(src, dst, ss.at[1], rs.at[1], device(x=left)))

    def forward_item(s):
        if s < CHUNKS:
            lo, hi = pl.ds(0, TOK // 2), pl.ds(TOK // 2, TOK // 2)
            a, b = token_piece(s, left, lo), token_piece(s, right, hi)
            ss, rs = ts.at[s], tr.at[s]
        else:
            c = s - CHUNKS
            a, b = weight_piece(c, left, 0, half // 2), weight_piece(c, right, half // 2, half // 2)
            ss, rs = ws.at[c], wr.at[c]
        return (send(a, a, ss.at[2], rs.at[2], device(x=right)), send(b, b, ss.at[3], rs.at[3], device(x=left)))

    first_hop, second_hop, to_core = {}, {}, {}
    first_hop[0] = send_item(0)
    k_copies = [send(kg.at[:, theirs], k_cat.at[:, :, pl.ds(128, 128)], ks.at[0], kr.at[0], device(yl=1 - yl))]
    for i, other in enumerate((right, left, across)):
        k_copies.append(send(kg.at[other, mine], k_rows.at[0, :, lanes(x)], ks.at[1 + 2 * i], kr.at[1 + 2 * i], device(x=other)))
        k_copies.append(send(kg.at[other, theirs], k_rows.at[1, :, lanes(x)], ks.at[2 + 2 * i], kr.at[2 + 2 * i], device(x=other)))
    first_hop[1] = send_item(1)

    def z_round(r):
        for step in (1 << r, -(1 << r)):
            pl.semaphore_signal(z_sem.at[r], inc=1, device_id=device(z=z_at(step)), device_id_type=MESH)

    z_round(0)

    def left_band(block):
        columns = block.shape[1]
        high, low = split(block)
        both = mm(left_w[...], jnp.concatenate([high, low], axis=1))
        return both[:64, :columns] + both[:64, columns:] + both[64:, :columns]

    def right_band(rows):
        both = mm(packed[pl.ds(0, rows)], right_w[...])
        return (both[:, :128] + both[:, 128:]).astype(BF)

    def inverse(coef, g):
        both = mm(coef, inv_right_w[:, pl.ds(pl.multiple_of(g * GROUP, GROUP), GROUP)])
        high, low = split(both[:, :128] + both[:, 128:])
        return mm(inv_left_w[...], jnp.concatenate([high, low, high], axis=0))

    def group_rows(c, g):
        return pl.ds(pl.multiple_of(c * width + g * GROUP, GROUP), GROUP)

    def group_lanes(g):
        return pl.ds(pl.multiple_of(g * GROUP, GROUP), GROUP)

    g_copies, p_copies = {}, {}

    def gradient_chunk(c):
        def body(g, carry):
            t = t_all[c, :, :, group_lanes(g)].reshape(N_X * TOK, GROUP)
            grad = mm(t, k_cat[...].reshape(N_X * TOK, 256), ((0,), (0,))) * (1.0 / 512)
            rows = pl.ds(pl.multiple_of(g * GROUP, GROUP), GROUP)
            g_send[c, rows] = grad[:, 128:].astype(BF)
            own = grad[:, :128] + DECAY * mom[group_rows(c, g)].astype(F32)
            g_own[c, rows] = own
            y = left_band(jnp.concatenate([own, grad[:, 128:]], axis=1))
            high, low = split(jnp.concatenate([y[:, :128], y[:, 128:]], axis=0))
            packed[:, group_lanes(g)] = jnp.concatenate([high, low], axis=1)
            return carry

        lax.fori_loop(0, groups, body, 0)
        g_copies[c] = send(g_send.at[c], g_recv.at[c], gs.at[c], gr.at[c], device(yl=1 - yl))
        coef = right_band(128)
        c_send[c, 0] = coef[:64]
        c_send[c, 1] = coef[64:]
        slot = yl * 4 + part
        send(c_send.at[c, 1], s1.at[slot], s1s.at[c, 1], s1r.at[slot], device(yl=1 - yl, yh=c // 2, core=c % 2))

        @pl.when(part != c)
        def _():
            own_coef_copy(c).start()

        @pl.when(part == c)
        def _():
            s1[slot] = c_send[c, 0]

    def own_coef_copy(c):
        slot = yl * 4 + part
        return pltpu.make_async_remote_copy(
            src_ref=c_send.at[c, 0], dst_ref=s1.at[slot], send_sem=s1s.at[c, 0], recv_sem=s1r.at[slot],
            device_id=device(yh=c // 2, core=c % 2), device_id_type=MESH,
        )

    def s1_copy(o):
        slot = (yl * 4 + part + o) % 8
        return pltpu.make_async_remote_copy(
            src_ref=c_send.at[0, 0], dst_ref=s1.at[slot], send_sem=s1s.at[0, 0], recv_sem=s1r.at[slot],
            device_id=device(yl=1 - yl), device_id_type=MESH,
        )

    def s2_copy(o):
        return pltpu.make_async_remote_copy(
            src_ref=s2.at[z], dst_ref=s2.at[z], send_sem=s2s.at[o], recv_sem=s2r.at[z],
            device_id=device(z=(z + o) % N_Z), device_id_type=MESH,
        )

    def s2_arrival(o):
        other = (z + o) % N_Z
        return pltpu.make_async_remote_copy(
            src_ref=s2.at[z], dst_ref=s2.at[other], send_sem=s2s.at[o], recv_sem=s2r.at[other],
            device_id=device(z=other), device_id_type=MESH,
        )

    def s3_copy(o):
        other = (part + o) % 4
        return pltpu.make_async_remote_copy(
            src_ref=s3.at[part], dst_ref=s3.at[part], send_sem=s3s.at[o], recv_sem=s3r.at[part],
            device_id=device(yh=other // 2, core=other % 2), device_id_type=MESH,
        )

    def s3_arrival(o):
        other = (part + o) % 4
        return pltpu.make_async_remote_copy(
            src_ref=s3.at[part], dst_ref=s3.at[other], send_sem=s3s.at[o], recv_sem=s3r.at[other],
            device_id=device(yh=other // 2, core=other % 2), device_id_type=MESH,
        )

    def repeat(first, last, act):
        lax.fori_loop(first, last, lambda o, carry: (act(o), carry)[1], 0)

    def reduce_near(c):
        @pl.when(part == c)
        def _():
            repeat(1, 8, lambda o: s1_copy(o).wait_recv())
            total = s1[0].astype(F32)
            for i in range(1, 8):
                total = total + s1[i].astype(F32)
            s2[z] = total.astype(BF)
            repeat(1, N_Z, lambda o: s2_copy(o).start())

    def reduce_far(c):
        @pl.when(part == c)
        def _():
            repeat(1, N_Z, lambda o: s2_arrival(o).wait_recv())
            total = s2[0].astype(F32)
            for i in range(1, N_Z):
                total = total + s2[i].astype(F32)
            s3[part] = total.astype(BF)
            repeat(1, 4, lambda o: s3_copy(o).start())

    def momentum_chunk(c):
        g_copies[c].wait_recv()

        def forward(g, carry):
            rows = pl.ds(pl.multiple_of(g * GROUP, GROUP), GROUP)
            moment = g_own[c, rows] + g_recv[c, rows].astype(F32)
            g_own[c, rows] = moment
            high, low = split(left_band(moment))
            packed[pl.ds(0, 64), group_lanes(g)] = jnp.concatenate([high, low], axis=1)
            return carry

        lax.fori_loop(0, groups, forward, 0)
        c_send_own = right_band(64)

        def back(g, carry):
            rows = pl.ds(pl.multiple_of(g * GROUP, GROUP), GROUP)
            new_mom[group_rows(c, g)] = (g_own[c, rows] - inverse(c_send_own, g)).astype(BF)
            return carry

        lax.fori_loop(0, groups, back, 0)

    def partial_chunk(c):
        for copy in to_core[c]:
            copy.wait_recv()

        def body(g, carry):
            p = mm(k_rows[...].reshape(2 * TOK, 512), w_all[group_rows(c, g)], ((1,), (1,)))
            p_own[c, :, group_lanes(g)] = p[:TOK]
            p_send[c, :, group_lanes(g)] = p[TOK:].astype(BF)
            return carry

        lax.fori_loop(0, groups, body, 0)
        p_copies[c] = send(p_send.at[c], p_recv.at[c], ps.at[c], pr.at[c], device(yl=1 - yl))

    other_core = device(core=1 - core)
    for copy in local:
        copy.wait()

    for s in range(2 * CHUNKS + 2):
        if s < 2 * CHUNKS:
            for copy in first_hop[s]:
                copy.wait_recv()
            second_hop[s] = forward_item(s)
            if s + 2 < 2 * CHUNKS:
                first_hop[s + 2] = send_item(s + 2)
            if s >= CHUNKS:
                c = s - CHUNKS
                to_core[c] = []
                for i, owner in enumerate((left, right)):
                    piece = weight_piece(c, owner)
                    to_core[c].append(send(piece, piece, cs.at[c, i], cr.at[c, i], other_core))
        if 1 <= s <= 2 * CHUNKS:
            for copy in second_hop[s - 1]:
                copy.wait_recv()
            if s - 1 >= CHUNKS:
                c = s - 1 - CHUNKS
                piece = weight_piece(c, across)
                to_core[c].append(send(piece, piece, cs.at[c, 2], cr.at[c, 2], other_core))
        if s == 1:
            for copy in k_copies:
                copy.wait_recv()
        if s < 3:
            pl.semaphore_wait(z_sem.at[s], 2)
            if s < 2:
                z_round(s + 1)
        if 1 <= s <= CHUNKS:
            gradient_chunk(s - 1)
        if 2 <= s <= CHUNKS + 1:
            reduce_near(s - 2)
        if s >= CHUNKS + 2:
            partial_chunk(s - CHUNKS - 2)
        if CHUNKS + 1 <= s <= 2 * CHUNKS:
            reduce_far(s - CHUNKS - 1)
        if s in (3, 5, 6, 8):
            momentum_chunk({3: 0, 5: 1, 6: 2, 8: 3}[s])

    for c in range(CHUNKS):
        p_copies[c].wait_recv()
        in_grad[:, pl.ds(c * width, width)] = (p_own[c] + p_recv[c].astype(F32)).astype(BF)

    repeat(1, 4, lambda o: s3_arrival(o).wait_recv())

    def finish(i, carry):
        c, g = i // groups, i % groups
        update[group_rows(c, g)] = inverse(s3[c], g).astype(BF)
        return carry

    lax.fori_loop(0, CHUNKS * groups, finish, 0)

    for copy in sent:
        copy.wait_send()
    for c in range(CHUNKS):

        @pl.when(part != c)
        def _():
            own_coef_copy(c).wait_send()

    repeat(1, N_Z, lambda o: s2_copy(o).wait_send())
    repeat(1, 4, lambda o: s3_copy(o).wait_send())


def cosine_table():
    freq = np.arange(SPAN, dtype=np.float64)[:, None]
    cell = np.arange(SPAN, dtype=np.float64)[None, :]
    scale = np.where(freq == 0.0, math.sqrt(1.0 / SPAN), math.sqrt(2.0 / SPAN))
    return (np.cos(math.pi * (2.0 * cell + 1.0) * freq / (2.0 * SPAN)) * scale).astype(np.float32)


def repeat_diagonal(block, count):
    eye = jnp.eye(count, dtype=F32)
    return (eye[:, None, :, None] * block[None, :, None, :]).reshape(count * block.shape[0], count * block.shape[1])


def bases(band_freqs):
    chosen = band_freqs[:, :, None] == jnp.arange(SPAN, dtype=jnp.int32)[None, None, :]
    basis = jnp.sum(jnp.where(chosen[..., None], cosine_table()[None, None], F32(0.0)), axis=2)
    high = lax.reduce_precision(basis, 8, 7)
    low = lax.reduce_precision(basis - high, 8, 7)
    row_high, row_low = repeat_diagonal(high[0], 4), repeat_diagonal(low[0], 4)
    left_w = jnp.concatenate([row_high, row_low], axis=0)
    inv_left_w = jnp.concatenate([row_high.T, row_high.T, row_low.T], axis=1)
    col_high, col_low = repeat_diagonal(high[1], 2), repeat_diagonal(low[1], 2)
    inv_right_w = repeat_diagonal(jnp.concatenate([col_high, col_low], axis=1), 4)
    high_t, low_t = col_high.T, col_low.T
    right_w = jnp.concatenate(
        [
            repeat_diagonal(jnp.concatenate([high_t, high_t], axis=0), 4),
            repeat_diagonal(jnp.concatenate([low_t, jnp.zeros_like(low_t)], axis=0), 4),
        ],
        axis=1,
    )
    return [w.astype(BF) for w in (left_w, right_w, inv_right_w, inv_left_w)]


def per_device(tokens, key_grad, key_weight, momentum, band_freqs):
    d_in = tokens.shape[1]
    width = d_in // CHUNKS
    vmem = pl.BlockSpec(memory_space=pltpu.VMEM)
    hbm = pl.BlockSpec(memory_space=pl.ANY)
    dma = pltpu.SemaphoreType.DMA
    new_momentum, update, input_grad = pl.pallas_call(
        kernel,
        out_shape=(
            jax.ShapeDtypeStruct((d_in, 128), BF),
            jax.ShapeDtypeStruct((d_in, 128), BF),
            jax.ShapeDtypeStruct((TOK, d_in), BF),
        ),
        in_specs=[hbm, vmem, hbm, vmem, vmem, vmem, vmem, vmem],
        out_specs=(vmem, vmem, vmem),
        scratch_shapes=[
            pltpu.VMEM((CHUNKS, N_X, TOK, width), BF),
            pltpu.VMEM((N_X, TOK, 256), BF),
            pltpu.VMEM((2, TOK, 512), BF),
            pltpu.VMEM((d_in, 512), BF),
            pltpu.VMEM((CHUNKS, width, 128), F32),
            pltpu.VMEM((CHUNKS, width, 128), BF),
            pltpu.VMEM((CHUNKS, width, 128), BF),
            pltpu.VMEM((CHUNKS, 2, 64, 128), BF),
            pltpu.VMEM((8, 64, 128), BF),
            pltpu.VMEM((N_Z, 64, 128), BF),
            pltpu.VMEM((4, 64, 128), BF),
            pltpu.VMEM((128, 4 * GROUP), BF),
            pltpu.VMEM((CHUNKS, TOK, width), F32),
            pltpu.VMEM((CHUNKS, TOK, width), BF),
            pltpu.VMEM((CHUNKS, TOK, width), BF),
            dma((4 + CHUNKS,)),
            dma((7,)),
            dma((7,)),
            dma((CHUNKS, 4)),
            dma((CHUNKS, 4)),
            dma((CHUNKS, 4)),
            dma((CHUNKS, 4)),
            dma((CHUNKS, 3)),
            dma((CHUNKS, 3)),
            dma((CHUNKS,)),
            dma((CHUNKS,)),
            dma((CHUNKS,)),
            dma((CHUNKS,)),
            dma((CHUNKS, 2)),
            dma((8,)),
            dma((N_Z,)),
            dma((N_Z,)),
            dma((4,)),
            dma((4,)),
            pltpu.SemaphoreType.REGULAR((3,)),
        ],
        compiler_params=pltpu.CompilerParams(
            collective_id=0, has_side_effects=True, vmem_limit_bytes=48 << 20
        ),
        name="band_step",
    )(tokens, key_grad.reshape(N_X, 2 * TOK, 128), key_weight, momentum[0], *bases(band_freqs))
    return new_momentum[None], update, input_grad


def solution(mesh):
    placed = (P(("dp", "mp"), None), P("dp", "mp"), P(None, "mp"), P("dp", None, "mp"), P())
    return jax.shard_map(
        per_device,
        mesh=mesh,
        in_specs=placed,
        out_specs=(P("dp", None, "mp"), P(None, "mp"), P(("dp", "mp"), None)),
        check_vma=False,
    )
```

time: 402 us -> 87 us (0.22)
  waiting for transfers between devices: 314 us -> 0 us
  Pallas kernels: 0 us -> 77.1 us
  matrix products: 32.1 us -> 0 us
  local copies, waits for them, and re-layouts: 28.9 us -> 5.6 us
  between operations: 13.9 us -> 0.8 us
  other arithmetic: 12.2 us -> 1.99 us
    all_gather x2 -> x0, waiting for transfers between devices: 241 us -> none  [the longest x1 138 us: per_device(): lax.all_gather(flat_band, 'dp', axis=0, tiled=True).astype(jnp.float32)]
    pallas_call x0 -> x1, Pallas kernels: none -> 77.1 us  [per_device(): pl.pallas_call(kernel, out_shape=(jax.ShapeDtypeStruct((d_in, 128), BF),...]
    reduce_scatter x1 -> x0, waiting for transfers between devices: 72.3 us -> none  [per_device(): lax.psum_scatter(lax.dot_general(key_rows, key_weight, (((1,), (1,)), (()...]
    dot_general x8 -> x0, matrix products: 32.1 us -> none  [the longest x2 15 us: inverse_band(): jnp.einsum('racj,jb->racb', left_done, col_basis, precision=exact_mode)]
    reshape x4 -> x0, local copies, waits for them, and re-layouts: 11 us -> none  [the longest x1 5.41 us: inverse_band(): return blocks.reshape(blocks.shape[0] * SPAN, blocks.shape[2] * SPAN)]
    reduce_sum x2 -> x1, other arithmetic: 9.2 us -> 1.11 us  [bases(): jnp.sum(jnp.where(chosen[..., None], cosine_table()[None, None], F32(0.0)...]
    dot_general x1 -> x0, local copies, waits for them, and re-layouts: 5.99 us -> none  [inverse_band(): jnp.einsum('racj,jb->racb', left_done, col_basis, precision=exact_mode)]
  transfers between devices with their start and end apart: 3 -> 0, of which waited for: 3 -> 0; matrix products, arithmetic and copies ran while one was open for 14% -> 0% of each run, Pallas kernels for 0% -> 0%
where the time goes in v1:
time: 87 us; the launch traced here: 85.5 us
  Pallas kernels  77.1 us (89%)
  local copies, waits for them, and re-layouts  5.6 us (6%)
  other arithmetic  1.99 us (2%)
    pallas_call x1, Pallas kernels, per_device(): pl.pallas_call(kernel, out_shape=(jax.ShapeDtypeStruct((d_in, 128), BF),...  77.1 us
    unnamed x14, local copies, waits for them, and re-layouts  4.53 us

profile of v1, /device:TPU:1, one launch (start us, length us, event | category | flops | bytes accessed | tf_op | source)
XLA Modules:
  0.0 85.5 jit_solution(927196252929472840)
XLA Ops:
  0.7 0.0 copy-start.3
  0.7 0.1 copy.22
  0.8 0.6 copy-done.3
  1.3 0.1 iota_compare_fusion
  1.4 1.1 %select_reduce_fusion = f32[2,16,64]{2,1,0:T(8,128)S(1)} fusion(f32[64,64]{1,0:T(8,128)} %constant.10, pred[2,16,64]{2,1,0:T(8,128)(4,1)S(1)} %iota_compare_fusion), kind=kLoop, calls=%fused_computation | loop fusion | flops 260096 | bytes 26624 | tf_op jit(solution)/shard_map/reduce_sum | solution.py:363
  2.6 0.1 broadcast_multiply_fusion.1
  2.6 0.1 mul.139
  2.7 0.1 mul.146
  2.8 0.1 multiply_convert_fusion.4
  3.0 0.1 reshape.69
  3.1 0.1 reshape.68
  3.2 0.1 copy.27
  3.3 0.1 copy.26
  3.4 0.1 pad_maximum_fusion.1.inv_left_w
  3.6 0.2 multiply_convert_fusion
  3.8 0.2 multiply_convert_fusion.2
  4.0 0.2 copy.23
  4.2 0.0 copy-start
  4.3 0.2 copy.24
  4.4 0.0 copy-start.1
  4.5 0.0 copy-start.2
  4.5 0.1 pad_maximum_fusion.right_w
  4.5 0.9 %copy-done = bf16[4096,128]{1,0:T(8,128)(2,1)S(1)} copy-done((bf16[4096,128]{1,0:T(8,128)(2,1)S(1)}, bf16[4096,128]{1,0:T(8,128)(2,1)}, u32[]{:S(2)}) %copy-start) | copy-done | bytes 1048600
  5.4 0.2 copy-done.1
  5.6 0.0 copy-done.2
  5.6 77.1 %band_step.1 = (bf16[4096,128]{1,0:T(8,128)(2,1)S(1)}, bf16[4096,128]{1,0:T(8,128)(2,1)S(1)}, bf16[64,4096]{1,0:T(8,128)(2,1)S(1)}) custom-call(bf16[64,4096]{1,0:T(8,128)(2,1)S(1)} %copy-done.1, bf16[4,128,128]{2,1,0:T(8,128)(2,1)S(1)} %bitcast.30, bf16[4096,128]{1,0:T(8,128)(2,1)S(1)} %copy-done, bf16[4096,128]{1,0:T(8,128)(2,1)} %bitcast.31, ...), custom_call_target="tpu_custom_call" | custom-call | tf_op jit(solution)/shard_map/band_step/pallas_call | solution.py:388
  82.7 1.0 %copy.34 = bf16[1,4096,128]{2,1,0:T(8,128)(2,1)} copy(bf16[1,4096,128]{2,1,0:T(8,128)(2,1)S(1)} %bitcast.29) | data formatting | bytes 2097152
  83.7 1.0 %copy.35 = bf16[4096,128]{1,0:T(8,128)(2,1)} copy(bf16[4096,128]{1,0:T(8,128)(2,1)S(1)} %get-tuple-element.27) | data formatting | bytes 2097152
  84.7 0.8 copy.36
  (11 shorter events, 0.1 us)
Async XLA Ops:
  0.7 0.7 copy-start.3
  4.2 1.2 %copy-start = (bf16[4096,128]{1,0:T(8,128)(2,1)S(1)}, bf16[4096,128]{1,0:T(8,128)(2,1)}, u32[]{:S(2)}) copy-start(bf16[4096,128]{1,0:T(8,128)(2,1)} %kw.1) | copy-start | bytes 3145732
  4.4 1.2 %copy-start.1 = (bf16[64,4096]{1,0:T(8,128)(2,1)S(1)}, bf16[64,4096]{1,0:T(8,128)(2,1)}, u32[]{:S(2)}) copy-start(bf16[64,4096]{1,0:T(8,128)(2,1)} %tok.1) | copy-start | bytes 1572868
  4.5 1.2 %copy-start.2 = (bf16[512,128]{1,0:T(8,128)(2,1)S(1)}, bf16[512,128]{1,0:T(8,128)(2,1)}, u32[]{:S(2)}) copy-start(bf16[512,128]{1,0:T(8,128)(2,1)} %param.7) | copy-start | bytes 393220

commit v2 on v1

--- a/solution.py
+++ b/solution.py
@@ -31,10 +31,11 @@
 
 
 def kernel(
-    tok, kg, kw, mom, left_w, right_w, inv_right_w, inv_left_w,
-    new_mom, update, in_grad,
+    tok, kg, kw, mom_hbm, freqs, cosines,
+    new_mom_hbm, update_hbm, in_grad_hbm,
+    new_mom, update, in_grad, mom, left_w, right_w, inv_right_w, inv_left_w,
     t_all, k_cat, k_rows, w_all, g_own, g_send, g_recv, c_send, s1, s2, s3, packed, p_own, p_send, p_recv,
-    loc_sem, ks, kr, ts, tr, ws, wr, cs, cr, gs, gr, ps, pr, s1s, s1r, s2s, s2r, s3s, s3r, z_sem,
+    loc_sem, ks, kr, ts, tr, ws, wr, cs, cr, gs, gr, ps, pr, s1s, s1r, s2s, s2r, s3s, s3r, z_sem, out_sem,
 ):
     width = t_all.shape[3]
     groups = width // GROUP
@@ -79,9 +80,10 @@
     local = [pltpu.make_async_copy(kg.at[:, mine], k_cat.at[:, :, pl.ds(0, 128)], loc_sem.at[0]),
              pltpu.make_async_copy(kg.at[x, mine], k_rows.at[0, :, lanes(x)], loc_sem.at[1]),
              pltpu.make_async_copy(kg.at[x, theirs], k_rows.at[1, :, lanes(x)], loc_sem.at[2]),
-             pltpu.make_async_copy(kw, w_all.at[:, lanes(x)], loc_sem.at[3])]
+             pltpu.make_async_copy(kw, w_all.at[:, lanes(x)], loc_sem.at[3]),
+             pltpu.make_async_copy(mom_hbm, mom, loc_sem.at[4])]
     for c in range(CHUNKS):
-        local.append(pltpu.make_async_copy(tok.at[:, pl.ds(c * width, width)], t_all.at[c, x], loc_sem.at[4 + c]))
+        local.append(pltpu.make_async_copy(tok.at[:, pl.ds(c * width, width)], t_all.at[c, x], loc_sem.at[5 + c]))
     for copy in local:
         copy.start()
     pl.semaphore_wait(barrier, len(near))
@@ -123,11 +125,40 @@
         k_copies.append(send(kg.at[other, theirs], k_rows.at[1, :, lanes(x)], ks.at[2 + 2 * i], kr.at[2 + 2 * i], device(x=other)))
     first_hop[1] = send_item(1)
 
+    def basis_weights():
+        def iota(shape, dim, shift, mask):
+            return (lax.broadcasted_iota(jnp.int32, shape, dim) >> shift) & mask
+
+        copies = iota((BAND, 128), 0, 0, 15) == iota((BAND, 128), 1, 0, 15)
+        spread = mm(freqs[...].astype(F32).astype(BF), copies.astype(F32).astype(BF))
+        freq = lax.broadcasted_iota(jnp.int32, (SPAN, 128), 0).astype(F32)
+        row_hot, col_hot = [(freq == spread[i : i + 1]).astype(F32).astype(BF) for i in range(2)]
+        high, low = cosines[0], cosines[1]
+        over = ((0,), (0,))
+        same = iota((64, 256), 0, 4, 3) == iota((64, 256), 1, 6, 3)
+        for i, table in enumerate((high, low)):
+            left_w[pl.ds(64 * i, 64)] = jnp.where(same, mm(row_hot, table, over)[:64], 0.0).astype(BF)
+        same = iota((256, 128), 0, 6, 3) == iota((256, 128), 1, 4, 3)
+        for i, table in enumerate((high, low)):
+            inv_left_w[:, pl.ds(128 * i, 128)] = jnp.where(same, mm(table, row_hot, over), 0.0).astype(BF)
+        both = mm(col_hot, jnp.concatenate([high[:, :128], low[:, :128]], axis=1), over)
+        block = iota((128, 256), 0, 4, 1) == iota((128, 256), 1, 6, 1)
+        for g in range(4):
+            kept = block & (iota((128, 256), 0, 5, 3) == g)
+            inv_right_w[:, pl.ds(GROUP * g, GROUP)] = jnp.where(kept, both, 0.0).astype(BF)
+        block = iota((256, 128), 0, 6, 1) == iota((256, 128), 1, 4, 1)
+        for i, table in enumerate((high, low)):
+            one = mm(table, col_hot, over)
+            for g in range(4):
+                kept = block & (iota((256, 128), 1, 5, 3) == g)
+                right_w[pl.ds(GROUP * g, GROUP), pl.ds(128 * i, 128)] = jnp.where(kept, one, 0.0).astype(BF)
+
     def z_round(r):
         for step in (1 << r, -(1 << r)):
             pl.semaphore_signal(z_sem.at[r], inc=1, device_id=device(z=z_at(step)), device_id_type=MESH)
 
     z_round(0)
+    basis_weights()
 
     def left_band(block):
         columns = block.shape[1]
@@ -142,7 +173,7 @@
     def inverse(coef, g):
         both = mm(coef, inv_right_w[:, pl.ds(pl.multiple_of(g * GROUP, GROUP), GROUP)])
         high, low = split(both[:, :128] + both[:, 128:])
-        return mm(inv_left_w[...], jnp.concatenate([high, low, high], axis=0))
+        return mm(inv_left_w[...], jnp.concatenate([high, low, high, low], axis=0))
 
     def group_rows(c, g):
         return pl.ds(pl.multiple_of(c * width + g * GROUP, GROUP), GROUP)
@@ -165,85 +196,87 @@
             packed[:, group_lanes(g)] = jnp.concatenate([high, low], axis=1)
             return carry
 
-        lax.fori_loop(0, groups, body, 0)
+        lax.fori_loop(0, groups, body, 0, unroll=True)
         g_copies[c] = send(g_send.at[c], g_recv.at[c], gs.at[c], gr.at[c], device(yl=1 - yl))
         coef = right_band(128)
         c_send[c, 0] = coef[:64]
         c_send[c, 1] = coef[64:]
-        slot = yl * 4 + part
-        send(c_send.at[c, 1], s1.at[slot], s1s.at[c, 1], s1r.at[slot], device(yl=1 - yl, yh=c // 2, core=c % 2))
-
-        @pl.when(part != c)
-        def _():
-            own_coef_copy(c).start()
-
-        @pl.when(part == c)
-        def _():
-            s1[slot] = c_send[c, 0]
-
-    def own_coef_copy(c):
-        slot = yl * 4 + part
-        return pltpu.make_async_remote_copy(
-            src_ref=c_send.at[c, 0], dst_ref=s1.at[slot], send_sem=s1s.at[c, 0], recv_sem=s1r.at[slot],
-            device_id=device(yh=c // 2, core=c % 2), device_id_type=MESH,
-        )
-
-    def s1_copy(o):
-        slot = (yl * 4 + part + o) % 8
-        return pltpu.make_async_remote_copy(
-            src_ref=c_send.at[0, 0], dst_ref=s1.at[slot], send_sem=s1s.at[0, 0], recv_sem=s1r.at[slot],
-            device_id=device(yl=1 - yl), device_id_type=MESH,
-        )
-
-    def s2_copy(o):
-        return pltpu.make_async_remote_copy(
-            src_ref=s2.at[z], dst_ref=s2.at[z], send_sem=s2s.at[o], recv_sem=s2r.at[z],
-            device_id=device(z=(z + o) % N_Z), device_id_type=MESH,
-        )
-
-    def s2_arrival(o):
-        other = (z + o) % N_Z
-        return pltpu.make_async_remote_copy(
-            src_ref=s2.at[z], dst_ref=s2.at[other], send_sem=s2s.at[o], recv_sem=s2r.at[other],
-            device_id=device(z=other), device_id_type=MESH,
-        )
-
-    def s3_copy(o):
-        other = (part + o) % 4
-        return pltpu.make_async_remote_copy(
-            src_ref=s3.at[part], dst_ref=s3.at[part], send_sem=s3s.at[o], recv_sem=s3r.at[part],
-            device_id=device(yh=other // 2, core=other % 2), device_id_type=MESH,
-        )
-
-    def s3_arrival(o):
-        other = (part + o) % 4
-        return pltpu.make_async_remote_copy(
-            src_ref=s3.at[part], dst_ref=s3.at[other], send_sem=s3s.at[o], recv_sem=s3r.at[other],
-            device_id=device(yh=other // 2, core=other % 2), device_id_type=MESH,
-        )
+        s1[c, slot] = c_send[c, 0, pl.ds(pl.multiple_of(part * BAND, BAND), BAND)]
+        repeat(1, 8, lambda o: s1_copy(c, o).start())
+
+    slot = yl * 4 + part
+    rows_of_part = pl.ds(pl.multiple_of(part * BAND, BAND), BAND)
 
     def repeat(first, last, act):
         lax.fori_loop(first, last, lambda o, carry: (act(o), carry)[1], 0)
 
+    def remote(src, dst, send_sem, recv_sem, to):
+        return pltpu.make_async_remote_copy(
+            src_ref=src, dst_ref=dst, send_sem=send_sem, recv_sem=recv_sem, device_id=to, device_id_type=MESH
+        )
+
+    def s1_copy(c, o):
+        to = (slot + o) % 8
+        to_yl, to_part = to // 4, to % 4
+        src = c_send.at[c, (to_yl + yl) % 2, pl.ds(pl.multiple_of(to_part * BAND, BAND), BAND)]
+        to_device = device(yl=to_yl, yh=to_part // 2, core=to_part % 2)
+        return remote(src, s1.at[c, slot], s1s.at[c], s1r.at[c], to_device)
+
+    def s2_copy(c, o):
+        return remote(s2.at[c, z], s2.at[c, z], s2s.at[c], s2r.at[c], device(z=(z + o) % N_Z))
+
+    def s3_copy(c, o):
+        to = (part + o) % 4
+        piece = s3.at[c, rows_of_part]
+        return remote(piece, piece, s3s.at[c], s3r.at[c], device(yh=to // 2, core=to % 2))
+
+    def all_of(ref, send_sem, recv_sem):
+        return remote(ref, ref, send_sem, recv_sem, device(core=1 - core))
+
+    def s1_all(c):
+        return all_of(s1.at[c, pl.ds(0, 7)], s1s.at[c], s1r.at[c])
+
+    def s2_all(c):
+        return all_of(s2.at[c, pl.ds(0, N_Z - 1)], s2s.at[c], s2r.at[c])
+
+    def s3_all(c):
+        return all_of(s3.at[c, pl.ds(0, 3 * BAND)], s3s.at[c], s3r.at[c])
+
     def reduce_near(c):
-        @pl.when(part == c)
-        def _():
-            repeat(1, 8, lambda o: s1_copy(o).wait_recv())
-            total = s1[0].astype(F32)
-            for i in range(1, 8):
-                total = total + s1[i].astype(F32)
-            s2[z] = total.astype(BF)
-            repeat(1, N_Z, lambda o: s2_copy(o).start())
+        s1_all(c).wait_recv()
+        total = s1[c, 0].astype(F32)
+        for i in range(1, 8):
+            total = total + s1[c, i].astype(F32)
+        s2[c, z] = total.astype(BF)
+        repeat(1, N_Z, lambda o: s2_copy(c, o).start())
 
     def reduce_far(c):
-        @pl.when(part == c)
-        def _():
-            repeat(1, N_Z, lambda o: s2_arrival(o).wait_recv())
-            total = s2[0].astype(F32)
-            for i in range(1, N_Z):
-                total = total + s2[i].astype(F32)
-            s3[part] = total.astype(BF)
-            repeat(1, 4, lambda o: s3_copy(o).start())
+        s2_all(c).wait_recv()
+        total = s2[c, 0].astype(F32)
+        for i in range(1, N_Z):
+            total = total + s2[c, i].astype(F32)
+        s3[c, rows_of_part] = total.astype(BF)
+        repeat(1, 4, lambda o: s3_copy(c, o).start())
+
+    written = []
+
+    def write(i, c, src, dst):
+        copy = pltpu.make_async_copy(src, dst, out_sem.at[i, c])
+        copy.start()
+        written.append(copy)
+
+    def chunk_rows(c):
+        return pl.ds(c * width, width)
+
+    def update_chunk(c):
+        s3_all(c).wait_recv()
+
+        def body(g, carry):
+            update[group_rows(c, g)] = inverse(s3[c], g).astype(BF)
+            return carry
+
+        lax.fori_loop(0, groups, body, 0, unroll=True)
+        write(1, c, update.at[chunk_rows(c)], update_hbm.at[chunk_rows(c)])
 
     def momentum_chunk(c):
         g_copies[c].wait_recv()
@@ -256,7 +289,7 @@
             packed[pl.ds(0, 64), group_lanes(g)] = jnp.concatenate([high, low], axis=1)
             return carry
 
-        lax.fori_loop(0, groups, forward, 0)
+        lax.fori_loop(0, groups, forward, 0, unroll=True)
         c_send_own = right_band(64)
 
         def back(g, carry):
@@ -264,7 +297,8 @@
             new_mom[group_rows(c, g)] = (g_own[c, rows] - inverse(c_send_own, g)).astype(BF)
             return carry
 
-        lax.fori_loop(0, groups, back, 0)
+        lax.fori_loop(0, groups, back, 0, unroll=True)
+        write(0, c, new_mom.at[chunk_rows(c)], new_mom_hbm.at[chunk_rows(c)])
 
     def partial_chunk(c):
         for copy in to_core[c]:
@@ -276,7 +310,7 @@
             p_send[c, :, group_lanes(g)] = p[TOK:].astype(BF)
             return carry
 
-        lax.fori_loop(0, groups, body, 0)
+        lax.fori_loop(0, groups, body, 0, unroll=True)
         p_copies[c] = send(p_send.at[c], p_recv.at[c], ps.at[c], pr.at[c], device(yl=1 - yl))
 
     other_core = device(core=1 - core)
@@ -318,32 +352,43 @@
             partial_chunk(s - CHUNKS - 2)
         if CHUNKS + 1 <= s <= 2 * CHUNKS:
             reduce_far(s - CHUNKS - 1)
-        if s in (3, 5, 6, 8):
-            momentum_chunk({3: 0, 5: 1, 6: 2, 8: 3}[s])
+        if s in (4, 5, 6, 8):
+            momentum_chunk({4: 0, 5: 1, 6: 2, 8: 3}[s])
+        if s >= CHUNKS + 3:
+            update_chunk(s - CHUNKS - 3)
 
     for c in range(CHUNKS):
         p_copies[c].wait_recv()
-        in_grad[:, pl.ds(c * width, width)] = (p_own[c] + p_recv[c].astype(F32)).astype(BF)
-
-    repeat(1, 4, lambda o: s3_arrival(o).wait_recv())
-
-    def finish(i, carry):
-        c, g = i // groups, i % groups
-        update[group_rows(c, g)] = inverse(s3[c], g).astype(BF)
-        return carry
-
-    lax.fori_loop(0, CHUNKS * groups, finish, 0)
-
+        in_grad[:, chunk_rows(c)] = (p_own[c] + p_recv[c].astype(F32)).astype(BF)
+        write(2, c, in_grad.at[:, chunk_rows(c)], in_grad_hbm.at[:, chunk_rows(c)])
+
+    update_chunk(CHUNKS - 1)
+
+    for copy in written:
+        copy.wait()
     for copy in sent:
         copy.wait_send()
     for c in range(CHUNKS):
-
-        @pl.when(part != c)
-        def _():
-            own_coef_copy(c).wait_send()
-
-    repeat(1, N_Z, lambda o: s2_copy(o).wait_send())
-    repeat(1, 4, lambda o: s3_copy(o).wait_send())
+        for copy in (s1_all(c), s2_all(c), s3_all(c)):
+            copy.wait_send()
+
+
+def hand_over(a, b, c, a_out, b_out, c_out, a_here, b_here, c_here, in_sem, out_sem):
+    arrays = ((a, a_here, a_out), (b, b_here, b_out), (c, c_here, c_out))
+    pieces = []
+    for i, (src, here, dst) in enumerate(arrays):
+        rows = src.shape[0] // 2
+        for j in range(2):
+            part = pl.ds(j * rows, rows)
+            first = pltpu.make_async_copy(src.at[part], here.at[part], in_sem.at[i, j])
+            second = pltpu.make_async_copy(here.at[part], dst.at[part], out_sem.at[i, j])
+            first.start()
+            pieces.append((first, second))
+    for first, second in pieces:
+        first.wait()
+        second.start()
+    for _, second in pieces:
+        second.wait()
 
 
 def cosine_table():
@@ -353,37 +398,18 @@
     return (np.cos(math.pi * (2.0 * cell + 1.0) * freq / (2.0 * SPAN)) * scale).astype(np.float32)
 
 
-def repeat_diagonal(block, count):
-    eye = jnp.eye(count, dtype=F32)
-    return (eye[:, None, :, None] * block[None, :, None, :]).reshape(count * block.shape[0], count * block.shape[1])
-
-
-def bases(band_freqs):
-    chosen = band_freqs[:, :, None] == jnp.arange(SPAN, dtype=jnp.int32)[None, None, :]
-    basis = jnp.sum(jnp.where(chosen[..., None], cosine_table()[None, None], F32(0.0)), axis=2)
-    high = lax.reduce_precision(basis, 8, 7)
-    low = lax.reduce_precision(basis - high, 8, 7)
-    row_high, row_low = repeat_diagonal(high[0], 4), repeat_diagonal(low[0], 4)
-    left_w = jnp.concatenate([row_high, row_low], axis=0)
-    inv_left_w = jnp.concatenate([row_high.T, row_high.T, row_low.T], axis=1)
-    col_high, col_low = repeat_diagonal(high[1], 2), repeat_diagonal(low[1], 2)
-    inv_right_w = repeat_diagonal(jnp.concatenate([col_high, col_low], axis=1), 4)
-    high_t, low_t = col_high.T, col_low.T
-    right_w = jnp.concatenate(
-        [
-            repeat_diagonal(jnp.concatenate([high_t, high_t], axis=0), 4),
-            repeat_diagonal(jnp.concatenate([low_t, jnp.zeros_like(low_t)], axis=0), 4),
-        ],
-        axis=1,
-    )
-    return [w.astype(BF) for w in (left_w, right_w, inv_right_w, inv_left_w)]
+def split_cosines():
+    table = cosine_table()
+    high = table.astype(BF)
+    low = (table - high.astype(np.float32)).astype(BF)
+    return np.stack([np.tile(high, (1, 4)), np.tile(low, (1, 4))])
 
 
 def per_device(tokens, key_grad, key_weight, momentum, band_freqs):
     d_in = tokens.shape[1]
     width = d_in // CHUNKS
     vmem = pl.BlockSpec(memory_space=pltpu.VMEM)
-    hbm = pl.BlockSpec(memory_space=pl.ANY)
+    hbm = pl.BlockSpec(memory_space=pltpu.HBM)
     dma = pltpu.SemaphoreType.DMA
     new_momentum, update, input_grad = pl.pallas_call(
         kernel,
@@ -392,9 +418,17 @@
             jax.ShapeDtypeStruct((d_in, 128), BF),
             jax.ShapeDtypeStruct((TOK, d_in), BF),
         ),
-        in_specs=[hbm, vmem, hbm, vmem, vmem, vmem, vmem, vmem],
-        out_specs=(vmem, vmem, vmem),
+        in_specs=[hbm, hbm, hbm, hbm, vmem, vmem],
+        out_specs=(hbm, hbm, hbm),
         scratch_shapes=[
+            pltpu.VMEM((d_in, 128), BF),
+            pltpu.VMEM((d_in, 128), BF),
+            pltpu.VMEM((TOK, d_in), BF),
+            pltpu.VMEM((d_in, 128), BF),
+            pltpu.VMEM((128, GROUP), BF),
+            pltpu.VMEM((4 * GROUP, 256), BF),
+            pltpu.VMEM((128, 4 * GROUP), BF),
+            pltpu.VMEM((GROUP, 256), BF),
             pltpu.VMEM((CHUNKS, N_X, TOK, width), BF),
             pltpu.VMEM((N_X, TOK, 256), BF),
             pltpu.VMEM((2, TOK, 512), BF),
@@ -403,14 +437,14 @@
             pltpu.VMEM((CHUNKS, width, 128), BF),
             pltpu.VMEM((CHUNKS, width, 128), BF),
             pltpu.VMEM((CHUNKS, 2, 64, 128), BF),
-            pltpu.VMEM((8, 64, 128), BF),
-            pltpu.VMEM((N_Z, 64, 128), BF),
-            pltpu.VMEM((4, 64, 128), BF),
+            pltpu.VMEM((CHUNKS, 8, BAND, 128), BF),
+            pltpu.VMEM((CHUNKS, N_Z, BAND, 128), BF),
+            pltpu.VMEM((CHUNKS, 64, 128), BF),
             pltpu.VMEM((128, 4 * GROUP), BF),
             pltpu.VMEM((CHUNKS, TOK, width), F32),
             pltpu.VMEM((CHUNKS, TOK, width), BF),
             pltpu.VMEM((CHUNKS, TOK, width), BF),
-            dma((4 + CHUNKS,)),
+            dma((5 + CHUNKS,)),
             dma((7,)),
             dma((7,)),
             dma((CHUNKS, 4)),
@@ -423,19 +457,29 @@
             dma((CHUNKS,)),
             dma((CHUNKS,)),
             dma((CHUNKS,)),
-            dma((CHUNKS, 2)),
-            dma((8,)),
-            dma((N_Z,)),
-            dma((N_Z,)),
-            dma((4,)),
-            dma((4,)),
+            dma((CHUNKS,)),
+            dma((CHUNKS,)),
+            dma((CHUNKS,)),
+            dma((CHUNKS,)),
+            dma((CHUNKS,)),
+            dma((CHUNKS,)),
             pltpu.SemaphoreType.REGULAR((3,)),
+            dma((3, CHUNKS)),
         ],
         compiler_params=pltpu.CompilerParams(
-            collective_id=0, has_side_effects=True, vmem_limit_bytes=48 << 20
+            collective_id=0, has_side_effects=True, vmem_limit_bytes=62 << 20
         ),
         name="band_step",
-    )(tokens, key_grad.reshape(N_X, 2 * TOK, 128), key_weight, momentum[0], *bases(band_freqs))
+    )(tokens, key_grad.reshape(N_X, 2 * TOK, 128), key_weight, momentum[0], band_freqs, split_cosines())
+    outs = (new_momentum, update, input_grad)
+    new_momentum, update, input_grad = pl.pallas_call(
+        hand_over,
+        out_shape=tuple(jax.ShapeDtypeStruct(o.shape, o.dtype) for o in outs),
+        in_specs=[pl.BlockSpec(memory_space=pl.ANY)] * 3,
+        out_specs=(hbm,) * 3,
+        scratch_shapes=[pltpu.VMEM(o.shape, o.dtype) for o in outs] + [dma((3, 2)), dma((3, 2))],
+        name="hand_over",
+    )(*outs)
     return new_momentum[None], update, input_grad
 
 

time: 87 us -> 73.2 us (0.84); the launches traced: 85.5 us -> 73 us
  local copies, waits for them, and re-layouts: 5.6 us -> 0 us
  Pallas kernels: 77.1 us -> 72.3 us
  other arithmetic: 1.99 us -> 0 us
    pallas_call x1, Pallas kernels: 77.1 us -> 69.7 us  [per_device(): pl.pallas_call(kernel, out_shape=(jax.ShapeDtypeStruct((d_in, 128), BF),...]
    unnamed x14 -> x0, local copies, waits for them, and re-layouts: 4.53 us -> none
    pallas_call x0 -> x1, Pallas kernels: none -> 2.63 us  [per_device(): pl.pallas_call(hand_over, out_shape=tuple((jax.ShapeDtypeStruct(o.shape,...]
    reduce_sum x1 -> x0, other arithmetic: 1.11 us -> none  [bases(): jnp.sum(jnp.where(chosen[..., None], cosine_table()[None, None], F32(0.0)...]
where the time goes in v2:
time: 73.2 us; the launch traced here: 73 us
  Pallas kernels  72.3 us (99%)
    pallas_call x1, Pallas kernels, per_device(): pl.pallas_call(kernel, out_shape=(jax.ShapeDtypeStruct((d_in, 128), BF),...  69.7 us
    pallas_call x1, Pallas kernels, per_device(): pl.pallas_call(hand_over, out_shape=tuple((jax.ShapeDtypeStruct(o.shape,...  2.63 us

profile of v2, /device:TPU:1, one launch (start us, length us, event | category | flops | bytes accessed | tf_op | source)
XLA Modules:
  0.0 73.0 jit_solution(4267349415009696677)
XLA Ops:
  0.6 69.7 %band_step.1 = (bf16[4096,128]{1,0:T(8,128)(2,1)}, bf16[4096,128]{1,0:T(8,128)(2,1)}, bf16[64,4096]{1,0:T(8,128)(2,1)}) custom-call(bf16[64,4096]{1,0:T(8,128)(2,1)} %tok.1, bf16[4,128,128]{2,1,0:T(8,128)(2,1)} %bitcast.4, bf16[4096,128]{1,0:T(8,128)(2,1)} %kw.1, bf16[4096,128]{1,0:T(8,128)(2,1)} %bitcast.3, s32[2,16]{1,0:T(2,128)} %freqs.1, ...), custom_call_target="tpu_custom_call" | custom-call | tf_op jit(solution)/shard_map/band_step/pallas_call | solution.py:414
  70.4 2.6 %hand_over.1 = (bf16[4096,128]{1,0:T(8,128)(2,1)}, bf16[4096,128]{1,0:T(8,128)(2,1)}, bf16[64,4096]{1,0:T(8,128)(2,1)}) custom-call(bf16[4096,128]{1,0:T(8,128)(2,1)} %get-tuple-element.9.a, bf16[4096,128]{1,0:T(8,128)(2,1)} %get-tuple-element.10.b, bf16[64,4096]{1,0:T(8,128)(2,1)} %get-tuple-element.11.c), custom_call_target="tpu_custom_call" | custom-call | tf_op jit(solution)/shard_map/hand_over/pallas_call | solution.py:475

commit v3 on v2

--- a/solution.py
+++ b/solution.py
@@ -197,12 +197,20 @@
             return carry
 
         lax.fori_loop(0, groups, body, 0, unroll=True)
-        g_copies[c] = send(g_send.at[c], g_recv.at[c], gs.at[c], gr.at[c], device(yl=1 - yl))
         coef = right_band(128)
         c_send[c, 0] = coef[:64]
         c_send[c, 1] = coef[64:]
         s1[c, slot] = c_send[c, 0, pl.ds(pl.multiple_of(part * BAND, BAND), BAND)]
         repeat(1, 8, lambda o: s1_copy(c, o).start())
+        if c == CHUNKS - 1:
+            send_gradient(c - 1, 1)
+        send_gradient(c, 0)
+        if c != CHUNKS - 2:
+            send_gradient(c, 1)
+
+    def send_gradient(c, i):
+        rows = pl.ds(i * width // 2, width // 2)
+        g_copies[c, i] = send(g_send.at[c, rows], g_recv.at[c, rows], gs.at[c, i], gr.at[c, i], device(yl=1 - yl))
 
     slot = yl * 4 + part
     rows_of_part = pl.ds(pl.multiple_of(part * BAND, BAND), BAND)
@@ -279,7 +287,8 @@
         write(1, c, update.at[chunk_rows(c)], update_hbm.at[chunk_rows(c)])
 
     def momentum_chunk(c):
-        g_copies[c].wait_recv()
+        for i in range(2):
+            g_copies[c, i].wait_recv()
 
         def forward(g, carry):
             rows = pl.ds(pl.multiple_of(g * GROUP, GROUP), GROUP)
@@ -453,8 +462,8 @@
             dma((CHUNKS, 4)),
             dma((CHUNKS, 3)),
             dma((CHUNKS, 3)),
-            dma((CHUNKS,)),
-            dma((CHUNKS,)),
+            dma((CHUNKS, 2)),
+            dma((CHUNKS, 2)),
             dma((CHUNKS,)),
             dma((CHUNKS,)),
             dma((CHUNKS,)),

time: 73.2 us -> 68.3 us (0.933)
  Pallas kernels: 72.3 us -> 67.5 us
    pallas_call x1, Pallas kernels: 69.7 us -> 64.9 us  [per_device(): pl.pallas_call(kernel, out_shape=(jax.ShapeDtypeStruct((d_in, 128), BF),...]
where the time goes in v3:
time: 68.3 us; the launch traced here: 68.1 us
  Pallas kernels  67.5 us (99%)
    pallas_call x1, Pallas kernels, per_device(): pl.pallas_call(kernel, out_shape=(jax.ShapeDtypeStruct((d_in, 128), BF),...  64.9 us
    pallas_call x1, Pallas kernels, per_device(): pl.pallas_call(hand_over, out_shape=tuple((jax.ShapeDtypeStruct(o.shape,...  2.63 us

profile of v3, /device:TPU:1, one launch (start us, length us, event | category | flops | bytes accessed | tf_op | source)
XLA Modules:
  0.0 68.1 jit_solution(2169257295736621135)
XLA Ops:
  0.6 64.9 %band_step.1 = (bf16[4096,128]{1,0:T(8,128)(2,1)}, bf16[4096,128]{1,0:T(8,128)(2,1)}, bf16[64,4096]{1,0:T(8,128)(2,1)}) custom-call(bf16[64,4096]{1,0:T(8,128)(2,1)} %tok.1, bf16[4,128,128]{2,1,0:T(8,128)(2,1)} %bitcast.4, bf16[4096,128]{1,0:T(8,128)(2,1)} %kw.1, bf16[4096,128]{1,0:T(8,128)(2,1)} %bitcast.3, s32[2,16]{1,0:T(2,128)} %freqs.1, ...), custom_call_target="tpu_custom_call" | custom-call | tf_op jit(solution)/shard_map/band_step/pallas_call | solution.py:423
  65.5 2.6 %hand_over.1 = (bf16[4096,128]{1,0:T(8,128)(2,1)}, bf16[4096,128]{1,0:T(8,128)(2,1)}, bf16[64,4096]{1,0:T(8,128)(2,1)}) custom-call(bf16[4096,128]{1,0:T(8,128)(2,1)} %get-tuple-element.9.a, bf16[4096,128]{1,0:T(8,128)(2,1)} %get-tuple-element.10.b, bf16[64,4096]{1,0:T(8,128)(2,1)} %get-tuple-element.11.c), custom_call_target="tpu_custom_call" | custom-call | tf_op jit(solution)/shard_map/hand_over/pallas_call | solution.py:484

commit v4 on v3

--- a/solution.py
+++ b/solution.py
@@ -15,10 +15,21 @@
 DECAY = 0.999
 N_X, N_Z = 4, 16
 CHUNKS = 4
+HALVES = 2 * CHUNKS
 GROUP = 256
 TOK = 64
 BF = jnp.bfloat16
 F32 = jnp.float32
+
+
+LATE = (
+    (("near", 2), ("mom", 1), ("near", 3)),
+    (("far", 0),),
+    (("far", 1), ("mom", 2)),
+    (("far", 2), ("far", 3), ("upd", 0)),
+    (("upd", 1), ("mom", 3)),
+    (("upd", 2), ("upd", 3)),
+)
 
 
 def split(value):
@@ -37,7 +48,7 @@
     t_all, k_cat, k_rows, w_all, g_own, g_send, g_recv, c_send, s1, s2, s3, packed, p_own, p_send, p_recv,
     loc_sem, ks, kr, ts, tr, ws, wr, cs, cr, gs, gr, ps, pr, s1s, s1r, s2s, s2r, s3s, s3r, z_sem, out_sem,
 ):
-    width = t_all.shape[3]
+    width = 2 * t_all.shape[3]
     groups = width // GROUP
     dp, mp = lax.axis_index("dp"), lax.axis_index("mp")
     yh, z, core = dp // 32, (dp // 2) % N_Z, dp % 2
@@ -82,13 +93,13 @@
              pltpu.make_async_copy(kg.at[x, theirs], k_rows.at[1, :, lanes(x)], loc_sem.at[2]),
              pltpu.make_async_copy(kw, w_all.at[:, lanes(x)], loc_sem.at[3]),
              pltpu.make_async_copy(mom_hbm, mom, loc_sem.at[4])]
-    for c in range(CHUNKS):
-        local.append(pltpu.make_async_copy(tok.at[:, pl.ds(c * width, width)], t_all.at[c, x], loc_sem.at[5 + c]))
+    half = width // 2
+    for h in range(HALVES):
+        local.append(pltpu.make_async_copy(tok.at[:, pl.ds(h * half, half)], t_all.at[h, x], loc_sem.at[5 + h]))
     for copy in local:
         copy.start()
     pl.semaphore_wait(barrier, len(near))
 
-    half = width // 2
 
     def token_piece(c, owner, rows=None):
         return t_all.at[c, owner] if rows is None else t_all.at[c, owner, rows]
@@ -98,21 +109,21 @@
         return w_all.at[pl.ds(first, count), lanes(owner)]
 
     def send_item(s):
-        if s < CHUNKS:
-            src, dst, ss, rs = tok.at[:, pl.ds(s * width, width)], token_piece(s, x), ts.at[s], tr.at[s]
+        if s < HALVES:
+            src, dst, ss, rs = tok.at[:, pl.ds(s * half, half)], token_piece(s, x), ts.at[s], tr.at[s]
         else:
-            c = s - CHUNKS
+            c = s - HALVES
             src = kw.at[pl.ds(pl.multiple_of(c * width + core * half, 16), half)]
             dst, ss, rs = weight_piece(c, x), ws.at[c], wr.at[c]
         return (send(src, dst, ss.at[0], rs.at[0], device(x=right)), send(src, dst, ss.at[1], rs.at[1], device(x=left)))
 
     def forward_item(s):
-        if s < CHUNKS:
+        if s < HALVES:
             lo, hi = pl.ds(0, TOK // 2), pl.ds(TOK // 2, TOK // 2)
             a, b = token_piece(s, left, lo), token_piece(s, right, hi)
             ss, rs = ts.at[s], tr.at[s]
         else:
-            c = s - CHUNKS
+            c = s - HALVES
             a, b = weight_piece(c, left, 0, half // 2), weight_piece(c, right, half // 2, half // 2)
             ss, rs = ws.at[c], wr.at[c]
         return (send(a, a, ss.at[2], rs.at[2], device(x=right)), send(b, b, ss.at[3], rs.at[3], device(x=left)))
@@ -124,6 +135,7 @@
         k_copies.append(send(kg.at[other, mine], k_rows.at[0, :, lanes(x)], ks.at[1 + 2 * i], kr.at[1 + 2 * i], device(x=other)))
         k_copies.append(send(kg.at[other, theirs], k_rows.at[1, :, lanes(x)], ks.at[2 + 2 * i], kr.at[2 + 2 * i], device(x=other)))
     first_hop[1] = send_item(1)
+    first_hop[2] = send_item(2)
 
     def basis_weights():
         def iota(shape, dim, shift, mask):
@@ -183,28 +195,31 @@
 
     g_copies, p_copies = {}, {}
 
-    def gradient_chunk(c):
-        def body(g, carry):
-            t = t_all[c, :, :, group_lanes(g)].reshape(N_X * TOK, GROUP)
+    def gradient_half(h):
+        c = h // 2
+        for i in range(groups // 2):
+            g = (h % 2) * (groups // 2) + i
+            t = t_all[h, :, :, group_lanes(i)].reshape(N_X * TOK, GROUP)
             grad = mm(t, k_cat[...].reshape(N_X * TOK, 256), ((0,), (0,))) * (1.0 / 512)
-            rows = pl.ds(pl.multiple_of(g * GROUP, GROUP), GROUP)
+            rows = pl.ds(g * GROUP, GROUP)
             g_send[c, rows] = grad[:, 128:].astype(BF)
             own = grad[:, :128] + DECAY * mom[group_rows(c, g)].astype(F32)
             g_own[c, rows] = own
             y = left_band(jnp.concatenate([own, grad[:, 128:]], axis=1))
             high, low = split(jnp.concatenate([y[:, :128], y[:, 128:]], axis=0))
             packed[:, group_lanes(g)] = jnp.concatenate([high, low], axis=1)
-            return carry
-
-        lax.fori_loop(0, groups, body, 0, unroll=True)
+        if h % 2 == 0:
+            if h < HALVES - 2:
+                send_gradient(c, 0)
+            return
         coef = right_band(128)
         c_send[c, 0] = coef[:64]
         c_send[c, 1] = coef[64:]
-        s1[c, slot] = c_send[c, 0, pl.ds(pl.multiple_of(part * BAND, BAND), BAND)]
+        s1[c, slot] = c_send[c, 0, rows_of_part]
         repeat(1, 8, lambda o: s1_copy(c, o).start())
         if c == CHUNKS - 1:
             send_gradient(c - 1, 1)
-        send_gradient(c, 0)
+            send_gradient(c, 0)
         if c != CHUNKS - 2:
             send_gradient(c, 1)
 
@@ -309,69 +324,82 @@
         lax.fori_loop(0, groups, back, 0, unroll=True)
         write(0, c, new_mom.at[chunk_rows(c)], new_mom_hbm.at[chunk_rows(c)])
 
-    def partial_chunk(c):
-        for copy in to_core[c]:
-            copy.wait_recv()
-
-        def body(g, carry):
+    def partial_half(c, i):
+        if i == 1:
+            for copy in to_core[c]:
+                copy.wait_recv()
+        which = core if i == 0 else 1 - core
+        for j in range(groups // 2):
+            g = which * (groups // 2) + j
             p = mm(k_rows[...].reshape(2 * TOK, 512), w_all[group_rows(c, g)], ((1,), (1,)))
             p_own[c, :, group_lanes(g)] = p[:TOK]
             p_send[c, :, group_lanes(g)] = p[TOK:].astype(BF)
-            return carry
-
-        lax.fori_loop(0, groups, body, 0, unroll=True)
-        p_copies[c] = send(p_send.at[c], p_recv.at[c], ps.at[c], pr.at[c], device(yl=1 - yl))
+        cols = pl.ds(pl.multiple_of(which * half, half), half)
+        p_copies[c, i] = send(p_send.at[c, :, cols], p_recv.at[c, :, cols], ps.at[c, i], pr.at[c, i], device(yl=1 - yl))
 
     other_core = device(core=1 - core)
     for copy in local:
         copy.wait()
 
-    for s in range(2 * CHUNKS + 2):
-        if s < 2 * CHUNKS:
-            for copy in first_hop[s]:
-                copy.wait_recv()
-            second_hop[s] = forward_item(s)
-            if s + 2 < 2 * CHUNKS:
-                first_hop[s + 2] = send_item(s + 2)
-            if s >= CHUNKS:
-                c = s - CHUNKS
-                to_core[c] = []
-                for i, owner in enumerate((left, right)):
-                    piece = weight_piece(c, owner)
-                    to_core[c].append(send(piece, piece, cs.at[c, i], cr.at[c, i], other_core))
-        if 1 <= s <= 2 * CHUNKS:
-            for copy in second_hop[s - 1]:
-                copy.wait_recv()
-            if s - 1 >= CHUNKS:
-                c = s - 1 - CHUNKS
-                piece = weight_piece(c, across)
-                to_core[c].append(send(piece, piece, cs.at[c, 2], cr.at[c, 2], other_core))
-        if s == 1:
+    def receive(s):
+        for copy in first_hop[s]:
+            copy.wait_recv()
+        second_hop[s] = forward_item(s)
+
+    def complete(s):
+        for copy in second_hop[s]:
+            copy.wait_recv()
+
+    for h in range(HALVES):
+        receive(h)
+        if h + 3 < HALVES:
+            first_hop[h + 3] = send_item(h + 3)
+        if h == HALVES - 1:
+            for c in range(2):
+                first_hop[HALVES + c] = send_item(HALVES + c)
+        if h == 1:
             for copy in k_copies:
                 copy.wait_recv()
-        if s < 3:
-            pl.semaphore_wait(z_sem.at[s], 2)
-            if s < 2:
-                z_round(s + 1)
-        if 1 <= s <= CHUNKS:
-            gradient_chunk(s - 1)
-        if 2 <= s <= CHUNKS + 1:
-            reduce_near(s - 2)
-        if s >= CHUNKS + 2:
-            partial_chunk(s - CHUNKS - 2)
-        if CHUNKS + 1 <= s <= 2 * CHUNKS:
-            reduce_far(s - CHUNKS - 1)
-        if s in (4, 5, 6, 8):
-            momentum_chunk({4: 0, 5: 1, 6: 2, 8: 3}[s])
-        if s >= CHUNKS + 3:
-            update_chunk(s - CHUNKS - 3)
+        if h >= 2:
+            complete(h - 2)
+            gradient_half(h - 2)
+        if h < 3:
+            pl.semaphore_wait(z_sem.at[h], 2)
+            if h < 2:
+                z_round(h + 1)
+        if h in (5, 7):
+            reduce_near(h // 2 - 2)
+        if h == 7:
+            momentum_chunk(0)
+    for h in (HALVES - 2, HALVES - 1):
+        complete(h)
+        gradient_half(h)
+
+    for w in range(CHUNKS + 2):
+        if w < CHUNKS:
+            receive(HALVES + w)
+            if w + 2 < CHUNKS:
+                first_hop[HALVES + w + 2] = send_item(HALVES + w + 2)
+            to_core[w] = []
+            for i, owner in enumerate((left, right)):
+                piece = weight_piece(w, owner)
+                to_core[w].append(send(piece, piece, cs.at[w, i], cr.at[w, i], other_core))
+        if 1 <= w <= CHUNKS:
+            complete(HALVES + w - 1)
+            piece = weight_piece(w - 1, across)
+            to_core[w - 1].append(send(piece, piece, cs.at[w - 1, 2], cr.at[w - 1, 2], other_core))
+        if w >= 2:
+            partial_half(w - 2, 1)
+        if 1 <= w <= CHUNKS:
+            partial_half(w - 1, 0)
+        for act in LATE[w]:
+            {"near": reduce_near, "far": reduce_far, "mom": momentum_chunk, "upd": update_chunk}[act[0]](act[1])
 
     for c in range(CHUNKS):
-        p_copies[c].wait_recv()
+        for i in range(2):
+            p_copies[c, i].wait_recv()
         in_grad[:, chunk_rows(c)] = (p_own[c] + p_recv[c].astype(F32)).astype(BF)
         write(2, c, in_grad.at[:, chunk_rows(c)], in_grad_hbm.at[:, chunk_rows(c)])
-
-    update_chunk(CHUNKS - 1)
 
     for copy in written:
         copy.wait()
@@ -438,7 +466,7 @@
             pltpu.VMEM((4 * GROUP, 256), BF),
             pltpu.VMEM((128, 4 * GROUP), BF),
             pltpu.VMEM((GROUP, 256), BF),
-            pltpu.VMEM((CHUNKS, N_X, TOK, width), BF),
+            pltpu.VMEM((HALVES, N_X, TOK, width // 2), BF),
             pltpu.VMEM((N_X, TOK, 256), BF),
             pltpu.VMEM((2, TOK, 512), BF),
             pltpu.VMEM((d_in, 512), BF),
@@ -453,19 +481,19 @@
             pltpu.VMEM((CHUNKS, TOK, width), F32),
             pltpu.VMEM((CHUNKS, TOK, width), BF),
             pltpu.VMEM((CHUNKS, TOK, width), BF),
-            dma((5 + CHUNKS,)),
+            dma((5 + HALVES,)),
             dma((7,)),
             dma((7,)),
-            dma((CHUNKS, 4)),
-            dma((CHUNKS, 4)),
+            dma((HALVES, 4)),
+            dma((HALVES, 4)),
             dma((CHUNKS, 4)),
             dma((CHUNKS, 4)),
             dma((CHUNKS, 3)),
             dma((CHUNKS, 3)),
             dma((CHUNKS, 2)),
             dma((CHUNKS, 2)),
-            dma((CHUNKS,)),
-            dma((CHUNKS,)),
+            dma((CHUNKS, 2)),
+            dma((CHUNKS, 2)),
             dma((CHUNKS,)),
             dma((CHUNKS,)),
             dma((CHUNKS,)),

time: 68.3 us -> 67.9 us (level)
  no operation moved by 1% of the time
where the time goes in v4:
time: 67.9 us; the launch traced here: 67.7 us
  Pallas kernels  67 us (99%)
    pallas_call x1, Pallas kernels, per_device(): pl.pallas_call(kernel, out_shape=(jax.ShapeDtypeStruct((d_in, 128), BF),...  64.4 us
    pallas_call x1, Pallas kernels, per_device(): pl.pallas_call(hand_over, out_shape=tuple((jax.ShapeDtypeStruct(o.shape,...  2.63 us

profile of v4, /device:TPU:1, one launch (start us, length us, event | category | flops | bytes accessed | tf_op | source)
XLA Modules:
  0.0 67.7 jit_solution(9858736572062945891)
XLA Ops:
  0.6 64.4 %band_step.1 = (bf16[4096,128]{1,0:T(8,128)(2,1)}, bf16[4096,128]{1,0:T(8,128)(2,1)}, bf16[64,4096]{1,0:T(8,128)(2,1)}) custom-call(bf16[64,4096]{1,0:T(8,128)(2,1)} %tok.1, bf16[4,128,128]{2,1,0:T(8,128)(2,1)} %bitcast.4, bf16[4096,128]{1,0:T(8,128)(2,1)} %kw.1, bf16[4096,128]{1,0:T(8,128)(2,1)} %bitcast.3, s32[2,16]{1,0:T(2,128)} %freqs.1, ...), custom_call_target="tpu_custom_call" | custom-call | tf_op jit(solution)/shard_map/band_step/pallas_call | solution.py:451
  65.1 2.6 %hand_over.1 = (bf16[4096,128]{1,0:T(8,128)(2,1)}, bf16[4096,128]{1,0:T(8,128)(2,1)}, bf16[64,4096]{1,0:T(8,128)(2,1)}) custom-call(bf16[4096,128]{1,0:T(8,128)(2,1)} %get-tuple-element.9.a, bf16[4096,128]{1,0:T(8,128)(2,1)} %get-tuple-element.10.b, bf16[64,4096]{1,0:T(8,128)(2,1)} %get-tuple-element.11.c), custom_call_target="tpu_custom_call" | custom-call | tf_op jit(solution)/shard_map/hand_over/pallas_call | solution.py:512
